TPU v7x, 32 devices: a whole 2x2x4 slice. The times are simulated.
32 devices in a mesh: group: 4 (over y, core), img: 8 (over z, x).
Axes of the slice: x: 2, y: 2, z: 4, core: 2. Of those that a mesh axis runs over, the one named last changes fastest.
Arguments:
- pixels: bfloat16 [32, 196, 8192], P(('group', 'img')), may hold values from -6 to 6
- band_mask: int32 [32, 32], P(('group', 'img')), may hold values from 0 to 1, as said below
- wavelength: int32 [4, 32], replicated, may hold values from 400 to 2499
- owner_order: int32 [7520], replicated, may hold values from 0 to 7519, as said below
- rest_weight: float32 [60160, 128], P(('group', 'img')), may hold values from -4 to 4, as said below
- rest_moment1: float32 [60160, 128], P(('group', 'img')), may hold values from -512 to 512
- rest_moment2: float32 [60160, 128], P(('group', 'img')), may hold values from 2090 to 8362
- fc_weight: float32 [128, 196608], P('group', 'img'), may hold values from -0.005859375 to 0.005859375
- fc_moment1: float32 [128, 196608], P('group', 'img'), may hold values from -2560 to 2560
- fc_moment2: float32 [128, 196608], P('group', 'img'), may hold values from 50176 to 200704
- cotangent: bfloat16 [6272, 768], P(('group', 'img')), may hold values from -6 to 6
Outputs:
- block_out: bfloat16 [6272, 768], P(('group', 'img'))
- pixel_grad: bfloat16 [32, 196, 8192], P(('group', 'img'))
- rest_new: float32 [60160, 128], P(('group', 'img'))
- rest_first: float32 [60160, 128], P(('group', 'img'))
- rest_second: float32 [60160, 128], P(('group', 'img'))
- fc_new: float32 [128, 196608], P('group', 'img')
- fc_first: float32 [128, 196608], P('group', 'img')
- fc_second: float32 [128, 196608], P('group', 'img')
Inputs may be any that keep to these rules, and one draw needn't show every extreme that they name: `band_mask`: every image has 2 to 32 present bands, and some image has all 32. `owner_order`: A permutation of the packed blocks. `rest_weight`: in the order given by owner_order; padding entries are zero and gains lie near 1.
All inputs are finite; a program needn't handle non-finite values.
Results may differ from a plain program's by a relative error of at most 0.019.
Values may be sent and summed in bfloat16 or wider, within the bound.
A program may use at most 320 MiB of HBM per device.

v0:
```python
import math

import jax
import jax.numpy as jnp
from jax import lax
from jax.sharding import PartitionSpec as P

D = 768
HEADS = 12
HD = 64
HID = 3072
E = 128
HH = 4
HFF = 2048
PATCH = 256
NB = 32
STEP = 5


beta_one = 0.5
beta_two = 0.75
decay_rate = 0.05
epsilon_add = 1e-08
rest_rate = 0.02


def for_sending(x):
    return jax.tree.map(lambda a: a.astype(jnp.bfloat16) if a.dtype == jnp.float32 else a, x)


def layout():
    return [
        ("w_qkv", (D, 3 * D)),
        ("w_out", (D, D)),
        ("w_up", (D, HID)),
        ("w_down", (HID, D)),
        ("h_query", (E, E)),
        ("h_key", (E, E)),
        ("h_value", (E, E)),
        ("h_out", (E, E)),
        ("h_ffin", (E, HFF)),
        ("h_ffout", (HFF, E)),
        ("ln1_gain", (D,)),
        ("ln1_shift", (D,)),
        ("ln2_gain", (D,)),
        ("ln2_shift", (D,)),
        ("patch_bias", (D,)),
        ("hn1_gain", (E,)),
        ("hn1_shift", (E,)),
        ("hn2_gain", (E,)),
        ("hn2_shift", (E,)),
    ]


def unpack(packed):
    params = {}
    offset = 0
    for entry_name, extent in layout():
        entry_size = math.prod(extent)
        params[entry_name] = packed[offset : offset + entry_size].reshape(extent)
        offset += entry_size
    return params


def layer_norm(values, gain, shift):
    center = values - jnp.mean(values, axis=-1, keepdims=True)
    spread = jnp.mean(center * center, axis=-1, keepdims=True)
    return center * lax.rsqrt(spread + 1e-06) * gain + shift


def exact_gelu(values):
    return jax.nn.gelu(values, approximate=False)


def embed_waves(wavelength):
    half_width = E // 2
    frequency = jnp.exp(-math.log(10000.0) * jnp.arange(half_width, dtype=jnp.float32) / half_width)
    angles = wavelength.astype(jnp.float32)[..., None] * frequency
    return jnp.concatenate([jnp.sin(angles), jnp.cos(angles)], axis=-1)


def hyper_layer(embedded, params):
    highest = lax.Precision.HIGHEST
    groups = embedded.shape[0]
    head_size = E // HH
    queries = jnp.einsum("gbe,ef->gbf", embedded, params["h_query"], precision=highest).reshape(
        groups, NB, HH, head_size
    )
    keys_h = jnp.einsum("gbe,ef->gbf", embedded, params["h_key"], precision=highest).reshape(
        groups, NB, HH, head_size
    )
    values_h = jnp.einsum("gbe,ef->gbf", embedded, params["h_value"], precision=highest).reshape(
        groups, NB, HH, head_size
    )
    scores = jnp.einsum("gbhc,gthc->ghbt", queries, keys_h, precision=highest) * head_size ** (-0.5)
    softmax_w = jax.nn.softmax(scores, axis=-1)
    mixed = jnp.einsum("ghbt,gthc->gbhc", softmax_w, values_h, precision=highest).reshape(
        groups, NB, E
    )
    attended = jnp.einsum("gbe,ef->gbf", mixed, params["h_out"], precision=highest)
    first_norm = layer_norm(embedded + attended, params["hn1_gain"], params["hn1_shift"])
    inner = jax.nn.gelu(
        jnp.einsum("gbe,ef->gbf", first_norm, params["h_ffin"], precision=highest),
        approximate=False,
    )
    outer = jnp.einsum("gbf,fe->gbe", inner, params["h_ffout"], precision=highest)
    second_norm = layer_norm(first_norm + outer, params["hn2_gain"], params["hn2_shift"])
    return second_norm + embedded


def block_pass(stream, weights, upstream):
    f32 = jnp.float32
    bf16 = jnp.bfloat16
    images, seq_len = (stream.shape[0], stream.shape[1])
    score_scale = HD ** (-0.5)
    gain_one = weights["ln1_gain"].astype(f32)
    shift_one = weights["ln1_shift"].astype(f32)
    gain_two = weights["ln2_gain"].astype(f32)
    shift_two = weights["ln2_shift"].astype(f32)
    first_f, norm_one_pull = jax.vjp(layer_norm, stream, gain_one, shift_one)
    first_norm = first_f.astype(bf16)
    qkv_joint = jnp.einsum(
        "isd,de->ise", first_norm, weights["w_qkv"], preferred_element_type=f32
    ).astype(bf16)
    qkv_split = qkv_joint.reshape(images, seq_len, 3, HEADS, HD)
    queries = qkv_split[:, :, 0]
    keys_h = qkv_split[:, :, 1]
    values_h = qkv_split[:, :, 2]
    scores = (
        jnp.einsum("ishd,ithd->ihst", queries, keys_h, preferred_element_type=f32) * score_scale
    )
    softmax_w = jax.nn.softmax(scores, axis=-1)
    softmax_low = softmax_w.astype(bf16)
    attended = (
        jnp.einsum("ihst,ithd->ishd", softmax_low, values_h, preferred_element_type=f32)
        .reshape(images, seq_len, D)
        .astype(bf16)
    )
    middle = stream + jnp.einsum(
        "isd,de->ise", attended, weights["w_out"], preferred_element_type=f32
    )
    second_f, norm_two_pull = jax.vjp(layer_norm, middle, gain_two, shift_two)
    second_norm = second_f.astype(bf16)
    hidden = jnp.einsum("isd,df->isf", second_norm, weights["w_up"], preferred_element_type=f32)
    activated_f, gelu_pull = jax.vjp(exact_gelu, hidden)
    activated = activated_f.astype(bf16)
    output = middle + jnp.einsum(
        "isf,fd->isd", activated, weights["w_down"], preferred_element_type=f32
    )
    grad_down = jnp.einsum("isf,isd->fd", activated, upstream, preferred_element_type=f32)
    grad_act = jnp.einsum("isd,fd->isf", upstream, weights["w_down"], preferred_element_type=f32)
    (grad_hidden_f,) = gelu_pull(grad_act)
    grad_hidden = grad_hidden_f.astype(bf16)
    grad_up = jnp.einsum("isd,isf->df", second_norm, grad_hidden, preferred_element_type=f32)
    grad_second = jnp.einsum(
        "isf,df->isd", grad_hidden, weights["w_up"], preferred_element_type=f32
    )
    grad_mid_norm, grad_gain_two, grad_shift_two = norm_two_pull(grad_second)
    grad_middle = upstream.astype(f32) + grad_mid_norm
    grad_mid_low = grad_middle.astype(bf16)
    grad_wout = jnp.einsum("isd,ise->de", attended, grad_mid_low, preferred_element_type=f32)
    grad_att = (
        jnp.einsum("ise,de->isd", grad_mid_low, weights["w_out"], preferred_element_type=f32)
        .astype(bf16)
        .reshape(images, seq_len, HEADS, HD)
    )
    grad_probs = jnp.einsum("ishd,ithd->ihst", grad_att, values_h, preferred_element_type=f32)
    grad_values = jnp.einsum("ihst,ishd->ithd", softmax_low, grad_att, preferred_element_type=f32)
    grad_scores = (
        softmax_w * (grad_probs - jnp.sum(softmax_w * grad_probs, axis=-1, keepdims=True))
    ).astype(bf16)
    grad_queries = (
        jnp.einsum("ihst,ithd->ishd", grad_scores, keys_h, preferred_element_type=f32) * score_scale
    )
    grad_keys = (
        jnp.einsum("ihst,ishd->ithd", grad_scores, queries, preferred_element_type=f32)
        * score_scale
    )
    grad_joint = (
        jnp.stack([grad_queries, grad_keys, grad_values], axis=2)
        .reshape(images, seq_len, 3 * D)
        .astype(bf16)
    )
    grad_qkv = jnp.einsum("isd,ise->de", first_norm, grad_joint, preferred_element_type=f32)
    grad_first = jnp.einsum("ise,de->isd", grad_joint, weights["w_qkv"], preferred_element_type=f32)
    grad_stream_norm, grad_gain_one, grad_shift_one = norm_one_pull(grad_first)
    grad_stream = grad_middle + grad_stream_norm
    grads = {
        "w_qkv": grad_qkv,
        "w_out": grad_wout,
        "w_up": grad_up,
        "w_down": grad_down,
        "ln1_gain": grad_gain_one,
        "ln1_shift": grad_shift_one,
        "ln2_gain": grad_gain_two,
        "ln2_shift": grad_shift_two,
    }
    return (output, grad_stream, grads)


def adamw_step(weight, moment_one, moment_two, grad, rate):
    first = beta_one * moment_one + (1.0 - beta_one) * grad
    second = beta_two * moment_two + (1.0 - beta_two) * grad * grad
    fix_one = 1.0 - beta_one**STEP
    fix_two = 1.0 - beta_two**STEP
    update = first / fix_one / (jnp.sqrt(second / fix_two) + epsilon_add) + decay_rate * weight
    return (weight - rate * update, first, second)


def on_device(
    pixels,
    band_mask,
    wavelength,
    owner_order,
    rest_weight,
    rest_moment1,
    rest_moment2,
    fc_weight,
    fc_moment1,
    fc_moment2,
    cotangent,
):
    f32 = jnp.float32
    bf16 = jnp.bfloat16
    kernel_rate = float(E * PATCH * NB) ** (-0.5)
    groups = lax.axis_size("group")
    images = pixels.shape[0]
    seq_len = pixels.shape[1]
    flat_width = pixels.shape[2]
    tok_rows = images * seq_len
    gathered = lax.all_gather(
        for_sending(rest_weight.astype(bf16)), ("group", "img"), axis=0, tiled=True
    )
    inverse = jnp.argsort(owner_order).astype(jnp.int32)
    packed = gathered.reshape(-1, 8, 128)[inverse].reshape(-1)
    weights = unpack(packed)
    hyper_names = [
        "h_query",
        "h_key",
        "h_value",
        "h_out",
        "h_ffin",
        "h_ffout",
        "hn1_gain",
        "hn1_shift",
        "hn2_gain",
        "hn2_shift",
    ]
    hyper_params = {entry_name: weights[entry_name].astype(f32) for entry_name in hyper_names}
    embedded = embed_waves(wavelength)

    def hyper_run(params_in):
        return hyper_layer(embedded, params_in)

    shaped, hyper_pull = jax.vjp(hyper_run, hyper_params)
    shaped_low = shaped.astype(bf16)
    band_width = E // groups
    group_id = lax.axis_index("group")
    own_shaped = lax.dynamic_slice_in_dim(shaped_low, group_id * band_width, band_width, 2)
    kernel_slab = fc_weight.astype(bf16).reshape(band_width, -1, PATCH)
    own_dims = kernel_slab.shape[1]
    chosen = lax.slice_in_dim(own_shaped, 0, 1 * lax.axis_size("group"), axis=0)
    kernel_own = lax.psum_scatter(
        jnp.einsum("gbk,kdp->gdbp", chosen, kernel_slab, preferred_element_type=f32).reshape(
            1 * lax.axis_size("group"), own_dims, flat_width
        ),
        "group",
        scatter_dimension=0,
        tiled=True,
    )
    kernel_low = kernel_own.reshape(own_dims, flat_width).astype(bf16)
    present = band_mask.astype(bf16)
    masked = (pixels.reshape(images, seq_len, NB, PATCH) * present[:, None, :, None]).reshape(
        tok_rows, flat_width
    )
    linear = lax.dot_general(
        masked,
        lax.all_gather(for_sending(kernel_low), "img", axis=0, tiled=True),
        (((1,), (1,)), ((), ())),
        preferred_element_type=f32,
    )
    stream = linear.reshape(images, seq_len, D) + weights["patch_bias"].astype(f32)
    upstream = cotangent.reshape(images, seq_len, D)
    output, grad_stream, block_grads = block_pass(stream, weights, upstream)
    grad_linear = grad_stream.reshape(tok_rows, D)
    grad_bias = jnp.sum(grad_linear, axis=0)
    grad_low = grad_linear.astype(bf16)
    piece_rows = jax.tree.map(
        lambda part: lax.all_gather(part, "img", axis=0, tiled=True), for_sending(kernel_low)
    )
    part_cols = lax.slice_in_dim(grad_low, 0, piece_rows.shape[0], axis=1)
    pixel_term = jnp.zeros((tok_rows, flat_width), f32) + jnp.dot(
        part_cols, piece_rows, preferred_element_type=f32
    )
    pixel_grad = (
        (pixel_term.reshape(images, seq_len, NB, PATCH) * present[:, None, :, None])
        .reshape(images, seq_len, flat_width)
        .astype(bf16)
    )
    part_cols = lax.slice_in_dim(grad_low, 0, own_dims * lax.axis_size("img"), axis=1)
    kernel_grad = lax.psum_scatter(
        lax.dot_general(part_cols, masked, (((0,), (0,)), ((), ())), preferred_element_type=f32),
        "img",
        scatter_dimension=0,
        tiled=True,
    )
    kernel_grad_low = kernel_grad.astype(bf16)
    all_groups = lax.all_gather(for_sending(kernel_grad_low[None]), "group", axis=0, tiled=True)
    grad_shape = all_groups.reshape(groups, own_dims, NB, PATCH)
    fc_grad = jnp.einsum(
        "gbk,gdbp->kdp", own_shaped, grad_shape, preferred_element_type=f32
    ).reshape(fc_weight.shape)
    shaped_part = jnp.einsum("gdbp,kdp->gbk", grad_shape, kernel_slab, preferred_element_type=f32)
    grad_shaped = lax.dynamic_update_slice_in_dim(
        jnp.zeros((groups, NB, E), f32), shaped_part, group_id * band_width, 2
    )
    (hyper_grads,) = hyper_pull(grad_shaped)
    all_grads = {}
    all_grads.update(block_grads)
    all_grads.update(hyper_grads)
    all_grads["patch_bias"] = grad_bias
    natural = jnp.concatenate(
        [all_grads[entry_name].reshape(-1) for entry_name, extent in layout()]
    )
    natural = jnp.concatenate(
        [natural, jnp.zeros((gathered.shape[0] * 128 - natural.shape[0],), f32)]
    )
    grad_blocks = natural.reshape(-1, 8, 128)
    own_rows = rest_weight.shape[0]
    joint_term = grad_blocks[owner_order].reshape(-1, 128)
    rest_grad = lax.psum_scatter(
        lax.slice_in_dim(joint_term, 0, own_rows * lax.axis_size(("group", "img")), axis=0),
        ("group", "img"),
        scatter_dimension=0,
        tiled=True,
    )
    rest_new, rest_first, rest_second = adamw_step(
        rest_weight, rest_moment1, rest_moment2, rest_grad, rest_rate
    )
    fc_new, fc_first, fc_second = adamw_step(
        fc_weight, fc_moment1, fc_moment2, fc_grad, kernel_rate
    )
    block_out = output.reshape(tok_rows, D).astype(bf16)
    return (block_out, pixel_grad, rest_new, rest_first, rest_second, fc_new, fc_first, fc_second)


def solution(mesh):
    placed = (
        P(("group", "img"), None, None),
        P(("group", "img"), None),
        P(),
        P(),
        P(("group", "img"), None),
        P(("group", "img"), None),
        P(("group", "img"), None),
        P("group", "img"),
        P("group", "img"),
        P("group", "img"),
        P(("group", "img"), None),
    )
    return jax.shard_map(
        on_device,
        mesh=mesh,
        in_specs=placed,
        out_specs=(
            P(("group", "img"), None),
            P(("group", "img"), None, None),
            P(("group", "img"), None),
            P(("group", "img"), None),
            P(("group", "img"), None),
            P("group", "img"),
            P("group", "img"),
            P("group", "img"),
        ),
        check_vma=False,
    )
```

profile of v0, /device:TPU:0, one launch (start us, length us, event | category | flops | bytes accessed | tf_op | source)
XLA Modules:
  0.0 1713.1 jit_solution(5230783193306386929)
XLA Ops:
  11.4 6.7 sort.17
  18.6 104.2 %all-gather.6.cloned.1.call-done = bf16[60160,128]{1,0:T(8,128)(2,1)} async-done(((bf16[1880,128]{1,0:T(8,128)(2,1)}), bf16[60160,128]{1,0:T(8,128)(2,1)}) %all-gather.6.cloned.1.call-update) | async-done | bytes 15400976 | tf_op jit(solution)/shard_map/all_gather | solution.py:231
  122.8 22.6 %gather_fusion = bf16[7520,8,128]{2,1,0:T(8,128)(2,1)} fusion(bf16[7520,8,128]{2,1,0:T(8,128)(2,1)} %bitcast.283, s32[8192]{0:T(1024)S(1)} %pad_clamp_fusion.1), kind=kCustom, calls=%fused_computation | custom fusion | bytes 30832000 | tf_op jit(solution)/shard_map/gather | solution.py:235
  160.3 6.3 convolution_bitcast_fusion.2
  166.6 13.8 reshape.712
  180.5 97.3 %reduce-scatter.7.cloned.1.call-done = f32[1,96,8192]{2,1,0:T(8,128)} async-done(((f32[4,96,8192]{2,1,0:T(8,128)}), f32[1,96,8192]{2,1,0:T(8,128)}) %reduce-scatter.7.cloned.1.call-update) | async-done | bytes 3145744 | tf_op jit(solution)/shard_map/reduce_scatter | solution.py:263
  294.8 8.3 fusion.110
  303.1 8.2 reshape.719
  311.3 9.3 reshape.720
  321.4 136.2 %all-gather.8.cloned.1.call-done = bf16[1,768,8192]{2,1,0:T(8,128)(2,1)} async-done(((bf16[1,96,8192]{2,1,0:T(8,128)(2,1)}), bf16[1,768,8192]{2,1,0:T(8,128)(2,1)}) %all-gather.8.cloned.1.call-update) | async-done | bytes 12582928 | tf_op jit(solution)/shard_map/all_gather | solution.py:278
  457.6 10.0 fusion.114
  476.6 7.1 multiply_convert_fusion.2
  504.9 8.0 reshape.722
  513.8 12.1 fusion.6
  548.9 10.9 reshape.725
  561.4 8.3 constant_dynamic-update-slice_fusion.11
  569.7 358.3 %reduce-scatter.9.cloned.1.call-done = f32[96,8192]{1,0:T(8,128)} async-done(((f32[768,8192]{1,0:T(8,128)}), f32[96,8192]{1,0:T(8,128)}) %reduce-scatter.9.cloned.1.call-update) | async-done | bytes 3145744 | tf_op jit(solution)/shard_map/reduce_scatter | solution.py:301
  931.3 8.4 constant_dynamic-update-slice_fusion.10
  939.7 37.2 %all-gather.10.cloned.1.call-done = bf16[384,8192]{1,0:T(8,128)(2,1)} async-done(((bf16[96,8192]{1,0:T(8,128)(2,1)}), bf16[384,8192]{1,0:T(8,128)(2,1)}) %all-gather.10.cloned.1.call-update) | async-done | bytes 6291472 | tf_op jit(solution)/shard_map/all_gather | solution.py:308
  1022.9 27.4 %gather_fusion.1 = f32[7520,8,128]{2,1,0:T(8,128)} fusion(f32[7520,8,128]{2,1,0:T(8,128)} %bitcast.280, s32[8192]{0:T(1024)S(1)} %copy-done.49), kind=kCustom, calls=%fused_computation.1 | custom fusion | bytes 61633920 | tf_op jit(solution)/shard_map/gather | solution.py:330
  1050.4 16.2 copy.83
  1066.6 8.6 multiply_convert_fusion
  1089.3 10.0 multiply_subtract_fusion
  1099.4 603.0 %reduce-scatter.11.cloned.1.call-done = f32[1880,128]{1,0:T(8,128)} async-done(((f32[60160,128]{1,0:T(8,128)}), f32[1880,128]{1,0:T(8,128)}) %reduce-scatter.11.cloned.1.call-update) | async-done | bytes 962576
  (325 shorter events, 158.8 us)
Async XLA Ops:
  7.2 115.7 %all-gather.6.cloned.1.call-start = ((), (), s32[]{:S(2)}) async-start(), calls=%async_computation.3 | async-start | bytes 15882240 | tf_op jit(solution)/shard_map/all_gather | solution.py:231
  9.3 268.5 %reduce-scatter.7.cloned.1.call-start = ((), (), s32[]{:S(2)}) async-start(), calls=%async_computation.4 | async-start | bytes 15728640 | tf_op jit(solution)/shard_map/reduce_scatter | solution.py:263
  11.4 148.9 %copy-start.3 = (bf16[32,24576]{1,0:T(8,128)(2,1)}, bf16[32,24576]{1,0:T(8,128)(2,1)S(1)}, u32[]{:S(2)}) copy-start(bf16[32,24576]{1,0:T(8,128)(2,1)S(1)} %convert_element_type.177) | copy-start | bytes 4718596
  18.6 132.3 %copy-start.16 = (f32[4,32,128]{2,1,0:T(8,128)}, f32[4,32,128]{2,1,0:T(8,128)S(1)}, u32[]{:S(2)}) copy-start(f32[4,32,128]{2,1,0:T(8,128)S(1)} %pad_maximum_fusion) | copy-start | bytes 196612
  180.4 100.7 %copy-start.82 = (s32[1,32]{1,0:T(1,128)S(1)}, s32[1,32]{1,0:T(1,128)}, u32[]{:S(2)}) copy-start(s32[1,32]{1,0:T(1,128)} %param.12) | copy-start | bytes 388
  180.4 277.2 %all-gather.8.cloned.1.call-start = ((), (), s32[]{:S(2)}) async-start(), calls=%async_computation.6 | async-start | bytes 14155776 | tf_op jit(solution)/shard_map/all_gather | solution.py:278
  281.0 647.0 %reduce-scatter.9.cloned.1.call-start = ((), (), s32[]{:S(2)}) async-start(), calls=%async_computation.5 | async-start | bytes 28311552 | tf_op jit(solution)/shard_map/reduce_scatter | solution.py:301
  311.3 9.3 copy-start.63
  457.6 10.2 copy-start.1
  476.3 60.2 %copy-start.8 = (f32[196,768]{1,0:T(8,128)}, f32[196,768]{1,0:T(8,128)S(1)}, u32[]{:S(2)}) copy-start(f32[196,768]{1,0:T(8,128)S(1)} %get-tuple-element.74) | copy-start | bytes 1806340
  504.9 8.0 copy-start.20
  513.8 12.1 copy-start.32
  525.9 451.0 %all-gather.10.cloned.1.call-start = ((), (), s32[]{:S(2)}) async-start(), calls=%async_computation.7 | async-start | bytes 7864320 | tf_op jit(solution)/shard_map/all_gather | solution.py:308
  548.9 10.9 copy-start.9
  931.3 771.2 %reduce-scatter.11.cloned.1.call-start = ((), (), s32[]{:S(2)}) async-start(), calls=%async_computation.8 | async-start | bytes 31764480
  1005.7 9.2 copy-start.68
  1005.7 10.5 copy-start.81
  1005.7 11.8 copy-start.80
  1005.7 17.2 %copy-start.49 = (s32[8192]{0:T(1024)S(1)}, s32[8192]{0:T(1024)}, u32[]{:S(2)}) copy-start(s32[8192]{0:T(1024)} %pad_clamp_fusion) | copy-start | bytes 98308
  1050.4 16.2 copy-start.33
  1050.4 16.2 copy-start.83
  1089.3 613.1 %copy-start.18 = (f32[1880,128]{1,0:T(8,128)S(1)}, f32[1880,128]{1,0:T(8,128)}, u32[]{:S(2)}) copy-start(f32[1880,128]{1,0:T(8,128)} %param.15) | copy-start | bytes 2887684
  1089.3 613.1 %copy-start.43 = (f32[1880,128]{1,0:T(8,128)S(1)}, f32[1880,128]{1,0:T(8,128)}, u32[]{:S(2)}) copy-start(f32[1880,128]{1,0:T(8,128)} %param.16) | copy-start | bytes 2887684
  1089.3 613.1 %copy-start.44 = (f32[1880,128]{1,0:T(8,128)S(1)}, f32[1880,128]{1,0:T(8,128)}, u32[]{:S(2)}) copy-start(f32[1880,128]{1,0:T(8,128)} %param.17) | copy-start | bytes 2887684
  (70 other events, 256.5 us)
Sparse Core Ops, SparseCore 0:
  11.4 111.3 all-gather.5
  180.5 97.2 reduce-scatter.6
  281.1 176.4 all-gather.7
  526.0 401.9 reduce-scatter.8
  931.4 45.4 all-gather.9
  1050.5 651.9 reduce-scatter.10
where the time goes:
time: 1720 us; the launch traced here: 1710 us
  waiting for transfers between devices  1340 us (78%)
  local copies, waits for them, and re-layouts  214 us (12%)
  matrix products  114 us (7%)
  other arithmetic  32.9 us (2%)
    unnamed x7, waiting for transfers between devices  603 us
    reduce_scatter x1, waiting for transfers between devices, on_device(): lax.psum_scatter(lax.dot_general(part_cols, masked, (((0,), (0,)), ((), (...  358 us
    all_gather x1, waiting for transfers between devices, on_device(): lax.all_gather(for_sending(kernel_low), 'img', axis=0, tiled=True)  136 us
    all_gather x1, waiting for transfers between devices, on_device(): lax.all_gather(for_sending(rest_weight.astype(bf16)), ('group', 'img'), a...  104 us
    reduce_scatter x1, waiting for transfers between devices, on_device(): lax.psum_scatter(jnp.einsum('gbk,kdp->gdbp', chosen, kernel_slab, preferr...  97.3 us
    unnamed x196, local copies, waits for them, and re-layouts  57.3 us
    all_gather x1, waiting for transfers between devices, on_device(): lax.all_gather(for_sending(kernel_grad_low[None]), 'group', axis=0, tiled...  37.2 us
  transfers between devices with their start and end apart: 6, of which 6 were waited for; matrix products, arithmetic and copies ran while one was open for 9% of the time, Pallas kernels for 0%

commit v1 on v0

v1 whole, which is shorter than its diff:
```python
import functools
import math

import jax
import jax.numpy as jnp
from jax import lax
from jax.experimental import pallas as pl
from jax.experimental.pallas import tpu as pltpu
from jax.sharding import PartitionSpec as P

MESH = pl.DeviceIdType.MESH

D = 768
HEADS = 12
HD = 64
HID = 3072
E = 128
HH = 4
HFF = 2048
PATCH = 256
NB = 32
STEP = 5


beta_one = 0.5
beta_two = 0.75
decay_rate = 0.05
epsilon_add = 1e-08
rest_rate = 0.02


def layout():
    return [
        ("w_qkv", (D, 3 * D)),
        ("w_out", (D, D)),
        ("w_up", (D, HID)),
        ("w_down", (HID, D)),
        ("h_query", (E, E)),
        ("h_key", (E, E)),
        ("h_value", (E, E)),
        ("h_out", (E, E)),
        ("h_ffin", (E, HFF)),
        ("h_ffout", (HFF, E)),
        ("ln1_gain", (D,)),
        ("ln1_shift", (D,)),
        ("ln2_gain", (D,)),
        ("ln2_shift", (D,)),
        ("patch_bias", (D,)),
        ("hn1_gain", (E,)),
        ("hn1_shift", (E,)),
        ("hn2_gain", (E,)),
        ("hn2_shift", (E,)),
    ]


def matrices():
    listed, at = [], 0
    for name, extent in layout():
        if len(extent) == 2:
            listed.append((name, extent[0], extent[1], at))
        at += math.prod(extent) // 128
    return listed


def vector_rows():
    first = sum(math.prod(extent) // 128 for _, extent in layout() if len(extent) == 2)
    count = sum(math.prod(extent) // 128 for _, extent in layout() if len(extent) == 1)
    return first, -(-count // 8) * 8


def spread_kernel(order_ref, low_ref, *refs):
    outs, linear = refs[:-1], refs[-1]
    step = pl.program_id(0)
    rows = low_ref.shape[0]

    def two(j, carry):
        pair = low_ref[pl.ds(pl.multiple_of(j * 16, 16), 16), :].astype(jnp.float32)
        for half in range(2):
            block = order_ref[step * (rows // 8) + j * 2 + half]
            linear[pl.ds(pl.multiple_of(block * 8, 8), 8), :] = pair[half * 8 : half * 8 + 8]
        return carry

    lax.fori_loop(0, rows // 16, two, 0, unroll=8)

    @pl.when(step == pl.num_programs(0) - 1)
    def _():
        for (name, height, width, first), out in zip(matrices(), outs):
            lanes = width // 128

            def some(j, carry, out=out, lanes=lanes, first=first):
                top = pl.multiple_of(j * 128, 128)
                for lane in range(lanes):
                    part = linear[pl.ds(first + top * lanes + lane, 128, stride=lanes), :]
                    out[pl.ds(top, 128), lane * 128 : lane * 128 + 128] = part.astype(out.dtype)
                return carry

            lax.fori_loop(0, height // 128, some, 0)
        first, count = vector_rows()
        outs[-1][...] = linear[first : first + count, :]


def spread_packed(gathered, slots, blocks):
    shards, rows = gathered.shape[0], gathered.shape[1]
    shapes = [
        jax.ShapeDtypeStruct((height, width), jnp.bfloat16 if name.startswith("w_") else jnp.float32)
        for name, height, width, first in matrices()
    ]
    shapes.append(jax.ShapeDtypeStruct((vector_rows()[1], 128), jnp.float32))
    return pl.pallas_call(
        spread_kernel,
        out_shape=shapes,
        grid_spec=pltpu.PrefetchScalarGridSpec(
            num_scalar_prefetch=1,
            grid=(shards,),
            in_specs=[pl.BlockSpec((None, rows, 128), lambda s, order: (s, 0, 0))],
            out_specs=[pl.BlockSpec(shape.shape, lambda s, order: (0, 0), pipeline_mode=pl.Buffered(1)) for shape in shapes],
            scratch_shapes=[pltpu.VMEM(((blocks + 1) * 8, 128), jnp.float32)],
        ),
        compiler_params=pltpu.CompilerParams(vmem_limit_bytes=60 << 20),
        name="spread_packed",
    )(slots, gathered)


def collect_kernel(order_ref, *refs):
    ins, low_ref, linear = refs[:-2], refs[-2], refs[-1]
    step = pl.program_id(0)
    rows = low_ref.shape[0]

    @pl.when(step == 0)
    def _():
        for (name, height, width, first), given in zip(matrices(), ins):
            lanes = width // 128

            def some(j, carry, given=given, lanes=lanes, first=first):
                top = pl.multiple_of(j * 128, 128)
                for lane in range(lanes):
                    part = given[pl.ds(top, 128), lane * 128 : lane * 128 + 128]
                    linear[pl.ds(first + top * lanes + lane, 128, stride=lanes), :] = part.astype(jnp.float32)
                return carry

            lax.fori_loop(0, height // 128, some, 0)
        first, count = vector_rows()
        linear[first : first + count, :] = ins[-1][...]
        rest = linear.shape[0] - first - count
        linear[first + count :, :] = jnp.zeros((rest, 128), jnp.float32)

    def two(j, carry):
        parts = []
        for half in range(2):
            block = order_ref[step * (rows // 8) + j * 2 + half]
            parts.append(linear[pl.ds(pl.multiple_of(block * 8, 8), 8), :])
        low_ref[pl.ds(pl.multiple_of(j * 16, 16), 16), :] = jnp.concatenate(parts, axis=0).astype(low_ref.dtype)
        return carry

    lax.fori_loop(0, rows // 16, two, 0, unroll=8)


def collect_packed(grads, slots, blocks, shards, rows):
    return pl.pallas_call(
        collect_kernel,
        out_shape=jax.ShapeDtypeStruct((shards, rows, 128), jnp.bfloat16),
        grid_spec=pltpu.PrefetchScalarGridSpec(
            num_scalar_prefetch=1,
            grid=(shards,),
            in_specs=[pl.BlockSpec(grad.shape, lambda s, order: (0, 0), pipeline_mode=pl.Buffered(1)) for grad in grads],
            out_specs=pl.BlockSpec((None, rows, 128), lambda s, order: (s, 0, 0)),
            scratch_shapes=[pltpu.VMEM(((blocks + 1) * 8, 128), jnp.float32)],
        ),
        compiler_params=pltpu.CompilerParams(vmem_limit_bytes=60 << 20),
        name="collect_packed",
    )(slots, *grads)


def layer_norm(values, gain, shift):
    center = values - jnp.mean(values, axis=-1, keepdims=True)
    spread = jnp.mean(center * center, axis=-1, keepdims=True)
    return center * lax.rsqrt(spread + 1e-06) * gain + shift


def embed_waves(wavelength):
    half_width = E // 2
    frequency = jnp.exp(-math.log(10000.0) * jnp.arange(half_width, dtype=jnp.float32) / half_width)
    angles = wavelength.astype(jnp.float32)[..., None] * frequency
    return jnp.concatenate([jnp.sin(angles), jnp.cos(angles)], axis=-1)


def hyper_layer(embedded, params):
    highest = lax.Precision.HIGHEST
    groups = embedded.shape[0]
    head_size = E // HH
    queries = jnp.einsum("gbe,ef->gbf", embedded, params["h_query"], precision=highest).reshape(
        groups, NB, HH, head_size
    )
    keys_h = jnp.einsum("gbe,ef->gbf", embedded, params["h_key"], precision=highest).reshape(
        groups, NB, HH, head_size
    )
    values_h = jnp.einsum("gbe,ef->gbf", embedded, params["h_value"], precision=highest).reshape(
        groups, NB, HH, head_size
    )
    scores = jnp.einsum("gbhc,gthc->ghbt", queries, keys_h, precision=highest) * head_size ** (-0.5)
    softmax_w = jax.nn.softmax(scores, axis=-1)
    mixed = jnp.einsum("ghbt,gthc->gbhc", softmax_w, values_h, precision=highest).reshape(
        groups, NB, E
    )
    attended = jnp.einsum("gbe,ef->gbf", mixed, params["h_out"], precision=highest)
    first_norm = layer_norm(embedded + attended, params["hn1_gain"], params["hn1_shift"])
    inner = jax.nn.gelu(
        jnp.einsum("gbe,ef->gbf", first_norm, params["h_ffin"], precision=highest),
        approximate=False,
    )
    outer = jnp.einsum("gbf,fe->gbe", inner, params["h_ffout"], precision=highest)
    second_norm = layer_norm(first_norm + outer, params["hn2_gain"], params["hn2_shift"])
    return second_norm + embedded


def tall(count):
    return -(-count // 16) * 16


def dot_nn(a, b):
    return lax.dot_general(a, b, (((1,), (0,)), ((), ())), preferred_element_type=jnp.float32)


def dot_nt(a, b):
    return lax.dot_general(a, b, (((1,), (1,)), ((), ())), preferred_element_type=jnp.float32)


def dot_tn(a, b):
    return lax.dot_general(a, b, (((0,), (0,)), ((), ())), preferred_element_type=jnp.float32)


def block_kernel(stream_ref, up_ref, vec_ref, wqkv_hbm, wout_hbm, wup_hbm, wdown_hbm,
                 out_ref, low_ref, gvec_ref, gqkv_hbm, gout_hbm, gup_hbm, gdown_hbm,
                 wqkv, wout, wup, wdown, gqkv, gout, gup, gdown,
                 xs, ups, up_low, norm_one, qkv, att, probs, mid, norm_two, acc, hid_low, datt, dqkv, in_sem, out_sem):
    f32, bf16 = jnp.float32, jnp.bfloat16
    seq = stream_ref.shape[0]
    rows = xs.shape[0]
    loads = [
        pltpu.make_async_copy(src, dst, in_sem.at[j])
        for j, (src, dst) in enumerate(((wqkv_hbm, wqkv), (wout_hbm, wout), (wup_hbm, wup), (wdown_hbm, wdown)))
    ]
    for load in loads:
        load.start()
    stores = [
        pltpu.make_async_copy(src, dst, out_sem.at[j])
        for j, (src, dst) in enumerate(((gqkv, gqkv_hbm), (gout, gout_hbm), (gup, gup_hbm), (gdown, gdown_hbm)))
    ]
    gain_one, shift_one = vec_ref[0:1, :], vec_ref[1:2, :]
    gain_two, shift_two = vec_ref[2:3, :], vec_ref[3:4, :]
    xs[...] = jnp.zeros_like(xs)
    xs[0:seq, :] = stream_ref[...] + vec_ref[4:5, :]
    ups[...] = jnp.zeros_like(ups)
    ups[0:seq, :] = up_ref[...].astype(f32)
    up_low[...] = ups[...].astype(bf16)

    def normed(values):
        center = values - jnp.mean(values, axis=-1, keepdims=True)
        scale = lax.rsqrt(jnp.mean(center * center, axis=-1, keepdims=True) + 1e-06)
        return center * scale, scale

    def normed_back(grad, unit, scale, gain):
        inner = grad * gain
        return scale * (
            inner
            - jnp.mean(inner, axis=-1, keepdims=True)
            - unit * jnp.mean(inner * unit, axis=-1, keepdims=True)
        )

    unit, scale = normed(xs[...])
    norm_one[...] = (unit * gain_one + shift_one).astype(bf16)
    loads[0].wait()

    def tile(j, size=D):
        return pl.ds(pl.multiple_of(j * size, size), size)

    def each(count, body):
        lax.fori_loop(0, count, lambda j, carry: (body(j), carry)[1], 0)

    def qkv_part(j):
        qkv[:, tile(j)] = dot_nn(norm_one[...], wqkv[:, tile(j)]).astype(bf16)

    each(3, qkv_part)
    inside = lax.broadcasted_iota(jnp.int32, (rows, rows), 1) < seq

    def heads(p):
        pair = [qkv[:, pl.ds(pl.multiple_of(j * D + p * 128, 128), 128)] for j in range(3)]
        outs = []
        for h in range(2):
            query, key, value = (part[:, h * HD : h * HD + HD] for part in pair)
            scores = jnp.where(inside, dot_nt(query, key) * (HD**-0.5), -1e30)
            weight = jnp.exp(scores - jnp.max(scores, axis=-1, keepdims=True))
            weight = weight / jnp.sum(weight, axis=-1, keepdims=True)
            probs[p * 2 + h] = weight
            outs.append(dot_nn(weight.astype(bf16), value))
        att[:, pl.ds(pl.multiple_of(p * 128, 128), 128)] = jnp.concatenate(outs, axis=1).astype(bf16)

    each(HEADS // 2, heads)
    loads[1].wait()
    mid[...] = xs[...] + dot_nn(att[...], wout[...])
    unit, scale = normed(mid[...])
    norm_two[...] = (unit * gain_two + shift_two).astype(bf16)
    loads[2].wait()
    loads[3].wait()
    acc[...] = jnp.zeros_like(acc)

    def hidden_part(j):
        hidden = dot_nn(norm_two[...], wup[:, tile(j)])
        half = 0.5 * (1.0 + lax.erf(hidden * (0.5**0.5)))
        active = (hidden * half).astype(bf16)
        slope = half + hidden * jnp.exp(-0.5 * hidden * hidden) * (2.0 * math.pi) ** -0.5
        mid[...] += dot_nn(active, wdown[tile(j), :])
        gdown[tile(j), :] = dot_tn(active, up_low[...]).astype(bf16)
        grad_hidden = (dot_nt(up_low[...], wdown[tile(j), :]) * slope).astype(bf16)
        gup[:, tile(j)] = dot_tn(norm_two[...], grad_hidden).astype(bf16)
        acc[...] += dot_nt(grad_hidden, wup[:, tile(j)])

    kept_unit, kept_scale = unit, scale
    hid_low[...] = kept_unit
    each(HID // D, hidden_part)
    stores[2].start()
    stores[3].start()
    out_ref[...] = mid[0:seq, :].astype(bf16)
    grad = acc[...]
    unit = hid_low[...]
    gvec_ref[...] = jnp.zeros_like(gvec_ref)
    gvec_ref[2:3, :] = jnp.sum(grad * unit, axis=0, keepdims=True)
    gvec_ref[3:4, :] = jnp.sum(grad, axis=0, keepdims=True)
    ups[...] += normed_back(grad, unit, kept_scale, gain_two)
    up_low[...] = ups[...].astype(bf16)
    gout[...] = dot_tn(att[...], up_low[...]).astype(bf16)
    stores[1].start()
    datt[...] = dot_nt(up_low[...], wout[...]).astype(bf16)

    def heads_back(p):
        pair = [qkv[:, pl.ds(pl.multiple_of(j * D + p * 128, 128), 128)] for j in range(3)]
        grad_pair = datt[:, pl.ds(pl.multiple_of(p * 128, 128), 128)]
        grads = [[], [], []]
        for h in range(2):
            query, key, value = (part[:, h * HD : h * HD + HD] for part in pair)
            grad_out = grad_pair[:, h * HD : h * HD + HD]
            weight = probs[p * 2 + h]
            grad_weight = dot_nt(grad_out, value)
            grads[2].append(dot_tn(weight.astype(bf16), grad_out))
            grad_score = weight * (grad_weight - jnp.sum(weight * grad_weight, axis=-1, keepdims=True))
            grad_score = grad_score.astype(bf16)
            grads[0].append(dot_nn(grad_score, key) * (HD**-0.5))
            grads[1].append(dot_tn(grad_score, query) * (HD**-0.5))
        for j in range(3):
            dqkv[:, pl.ds(pl.multiple_of(j * D + p * 128, 128), 128)] = jnp.concatenate(grads[j], axis=1).astype(bf16)

    each(HEADS // 2, heads_back)
    acc[...] = jnp.zeros_like(acc)

    def qkv_back(j):
        gqkv[:, tile(j)] = dot_tn(norm_one[...], dqkv[:, tile(j)]).astype(bf16)
        acc[...] += dot_nt(dqkv[:, tile(j)], wqkv[:, tile(j)])

    each(3, qkv_back)
    stores[0].start()
    unit, scale = normed(xs[...])
    grad = acc[...]
    gvec_ref[0:1, :] = jnp.sum(grad * unit, axis=0, keepdims=True)
    gvec_ref[1:2, :] = jnp.sum(grad, axis=0, keepdims=True)
    total = ups[...] + normed_back(grad, unit, scale, gain_one)
    gvec_ref[4:5, :] = jnp.sum(total, axis=0, keepdims=True)
    low_ref[...] = total.astype(bf16)
    for store in stores:
        store.wait()


def block_pass(stream, upstream, vectors, wqkv, wout, wup, wdown):
    f32, bf16 = jnp.float32, jnp.bfloat16
    seq = stream.shape[0]
    rows = tall(seq)
    whole = pl.BlockSpec(memory_space=pltpu.VMEM)
    far = pl.BlockSpec(memory_space=pl.ANY)
    mats = [wqkv, wout, wup, wdown]
    kept = [pltpu.VMEM(mat.shape, bf16) for mat in mats]
    dma = pltpu.SemaphoreType.DMA
    return pl.pallas_call(
        block_kernel,
        out_shape=[
            jax.ShapeDtypeStruct((seq, D), bf16),
            jax.ShapeDtypeStruct((rows, D), bf16),
            jax.ShapeDtypeStruct((8, D), f32),
        ]
        + [jax.ShapeDtypeStruct(mat.shape, bf16) for mat in mats],
        in_specs=[whole] * 3 + [far] * 4,
        out_specs=[whole] * 3 + [far] * 4,
        scratch_shapes=kept
        + kept
        + [
            pltpu.VMEM((rows, D), f32),
            pltpu.VMEM((rows, D), f32),
            pltpu.VMEM((rows, D), bf16),
            pltpu.VMEM((rows, D), bf16),
            pltpu.VMEM((rows, 3 * D), bf16),
            pltpu.VMEM((rows, D), bf16),
            pltpu.VMEM((HEADS, rows, rows), f32),
            pltpu.VMEM((rows, D), f32),
            pltpu.VMEM((rows, D), bf16),
            pltpu.VMEM((rows, D), f32),
            pltpu.VMEM((rows, D), f32),
            pltpu.VMEM((rows, D), bf16),
            pltpu.VMEM((rows, 3 * D), bf16),
            dma((4,)),
            dma((4,)),
        ],
        compiler_params=pltpu.CompilerParams(vmem_limit_bytes=60 << 20),
        cost_estimate=pl.CostEstimate(flops=8_400_000_000, bytes_accessed=30_000_000, transcendentals=2_000_000),
        name="block_pass",
    )(stream, upstream, vectors, *mats)


def adamw_step(weight, moment_one, moment_two, grad, rate):
    first = beta_one * moment_one + (1.0 - beta_one) * grad
    second = beta_two * moment_two + (1.0 - beta_two) * grad * grad
    fix_one = 1.0 - beta_one**STEP
    fix_two = 1.0 - beta_two**STEP
    update = first / fix_one / (jnp.sqrt(second / fix_two) + epsilon_add) + decay_rate * weight
    return (weight - rate * update, first, second)


NC = 8


def dims_step(count):
    return 16 if count % 16 == 0 else count


def make_kernel(shaped_ref, master_ref, kernel_ref, turned):
    dims = kernel_ref.shape[0]
    for dim in range(dims):
        part = dot_nn(shaped_ref[...], master_ref[:, dim * PATCH : (dim + 1) * PATCH])
        turned[pl.ds(dim, NB, stride=dims), :] = part[:, :128]
        turned[pl.ds(NB * dims + dim, NB, stride=dims), :] = part[:, 128:]
    for band in range(NB):
        for half in range(2):
            row = half * NB * dims + band * dims
            lane = band * PATCH + half * 128
            kernel_ref[:, lane : lane + 128] = turned[row : row + dims, :].astype(kernel_ref.dtype)


def make_kernels(shaped, master):
    dims = master.shape[1] // PATCH
    step = dims_step(dims)
    return pl.pallas_call(
        make_kernel,
        out_shape=jax.ShapeDtypeStruct((dims, NB * PATCH), jnp.bfloat16),
        grid=(dims // step,),
        in_specs=[
            pl.BlockSpec(shaped.shape, lambda j: (0, 0)),
            pl.BlockSpec((E, step * PATCH), lambda j: (0, j)),
        ],
        out_specs=pl.BlockSpec((step, NB * PATCH), lambda j: (j, 0)),
        scratch_shapes=[pltpu.VMEM((2 * NB * step, 128), jnp.float32)],
        compiler_params=pltpu.CompilerParams(vmem_limit_bytes=60 << 20),
        name="make_kernels",
    )(shaped, master)


def embed_kernel(pixel_ref, mask_ref, kernel_ref, stream_ref):
    masked = pixel_ref[...] * mask_ref[...].astype(jnp.bfloat16)
    part = dot_nt(masked, kernel_ref[...])

    @pl.when(pl.program_id(0) == 0)
    def _():
        stream_ref[...] = part

    @pl.when(pl.program_id(0) > 0)
    def _():
        stream_ref[...] += part


def embed_patches(pixels, mask, kernels):
    seq, width = pixels.shape[1], pixels.shape[2]
    cut = 1024
    return pl.pallas_call(
        embed_kernel,
        out_shape=jax.ShapeDtypeStruct((seq, D), jnp.float32),
        grid=(width // cut,),
        in_specs=[
            pl.BlockSpec((None, seq, cut), lambda j: (0, 0, j)),
            pl.BlockSpec((1, cut), lambda j: (0, j)),
            pl.BlockSpec((D, cut), lambda j: (0, j)),
        ],
        out_specs=pl.BlockSpec((seq, D), lambda j: (0, 0)),
        compiler_params=pltpu.CompilerParams(vmem_limit_bytes=60 << 20),
        name="embed_patches",
    )(pixels, mask, kernels)


def unembed_kernel(pixel_ref, mask_ref, kernel_ref, low_ref, back_ref, grad_ref, masked):
    seq = pixel_ref.shape[0]
    mask = mask_ref[...]
    masked[...] = jnp.zeros_like(masked)
    masked[0:seq, :] = pixel_ref[...].astype(jnp.float32) * mask
    back_ref[...] = (dot_nn(low_ref[...], kernel_ref[...])[0:seq] * mask).astype(back_ref.dtype)
    grad_ref[...] = dot_tn(low_ref[...], masked[...].astype(jnp.bfloat16)).astype(grad_ref.dtype)


def unembed_patches(pixels, mask, kernels, low):
    seq, width = pixels.shape[1], pixels.shape[2]
    cut = 1024
    return pl.pallas_call(
        unembed_kernel,
        out_shape=[
            jax.ShapeDtypeStruct(pixels.shape, jnp.bfloat16),
            jax.ShapeDtypeStruct((D, width), jnp.bfloat16),
        ],
        grid=(width // cut,),
        in_specs=[
            pl.BlockSpec((None, seq, cut), lambda j: (0, 0, j)),
            pl.BlockSpec((1, cut), lambda j: (0, j)),
            pl.BlockSpec((D, cut), lambda j: (0, j)),
            pl.BlockSpec(low.shape, lambda j: (0, 0)),
        ],
        out_specs=[
            pl.BlockSpec((None, seq, cut), lambda j: (0, 0, j)),
            pl.BlockSpec((D, cut), lambda j: (0, j)),
        ],
        scratch_shapes=[pltpu.VMEM((low.shape[0], cut), jnp.float32)],
        compiler_params=pltpu.CompilerParams(vmem_limit_bytes=60 << 20),
        name="unembed_patches",
    )(pixels, mask, kernels, low)


def master_kernel(rate, grad_ref, shaped_ref, weight_ref, one_ref, two_ref, new_ref, first_ref, second_ref, back_ref, turned):
    groups, dims = grad_ref.shape[0], grad_ref.shape[1]
    bands = groups * NB
    for group in range(groups):
        for band in range(NB):
            for half in range(2):
                row = half * bands * dims + (group * NB + band) * dims
                lane = band * PATCH + half * 128
                turned[row : row + dims, :] = grad_ref[group, :, lane : lane + 128].astype(jnp.float32)
    total = jnp.zeros(back_ref.shape, jnp.float32)
    for dim in range(dims):
        part = jnp.concatenate(
            [turned[pl.ds(half * bands * dims + dim, bands, stride=dims), :] for half in range(2)], axis=1
        ).astype(jnp.bfloat16)
        lanes = slice(dim * PATCH, (dim + 1) * PATCH)
        weight = weight_ref[:, lanes]
        total += dot_nt(part, weight.astype(jnp.bfloat16))
        grad = dot_tn(shaped_ref[...], part)
        new_ref[:, lanes], first_ref[:, lanes], second_ref[:, lanes] = adamw_step(
            weight, one_ref[:, lanes], two_ref[:, lanes], grad, rate
        )

    @pl.when(pl.program_id(0) == 0)
    def _():
        back_ref[...] = total

    @pl.when(pl.program_id(0) > 0)
    def _():
        back_ref[...] += total


def master_update(grads, shaped, weight, one, two, rate):
    groups, dims = grads.shape[0], grads.shape[1]
    step = dims_step(dims)
    columns = pl.BlockSpec((weight.shape[0], step * PATCH), lambda j: (0, j))
    like = jax.ShapeDtypeStruct(weight.shape, jnp.float32)
    return pl.pallas_call(
        functools.partial(master_kernel, rate),
        out_shape=[like, like, like, jax.ShapeDtypeStruct(shaped.shape, jnp.float32)],
        grid=(dims // step,),
        in_specs=[
            pl.BlockSpec((groups, step, NB * PATCH), lambda j: (0, j, 0)),
            pl.BlockSpec(shaped.shape, lambda j: (0, 0)),
            columns,
            columns,
            columns,
        ],
        out_specs=[columns, columns, columns, pl.BlockSpec(shaped.shape, lambda j: (0, 0))],
        scratch_shapes=[pltpu.VMEM((2 * groups * NB * step, 128), jnp.float32)],
        compiler_params=pltpu.CompilerParams(vmem_limit_bytes=60 << 20),
        name="master_update",
    )(grads, shaped, weight, one, two)


def spot():
    group = lax.axis_index("group")
    image = lax.axis_index("img")
    return group // 2, group % 2, image // 2, image % 2


def place(y, c, z, x):
    return (y * 2 + c, z * 2 + x)


def partners():
    y, c, z, x = spot()
    x2, y2 = x + (1 - c) * (1 - 2 * x), y + c * (1 - 2 * y)
    x3, y3 = x + c * (1 - 2 * x), y + (1 - c) * (1 - 2 * y)
    around = [place(y, c, (z + d) % 4, x) for d in (1, 2, 3)]
    return (x2, y2), (x3, y3), around, place(y2, c, z, x2), place(y3, c, z, x3), place(y, 1 - c, z, x)


def greet(peers):
    barrier = pltpu.get_barrier_semaphore()
    for peer in peers:
        pl.semaphore_signal(barrier, inc=1, device_id=peer, device_id_type=MESH)
    pl.semaphore_wait(barrier, len(peers))


def gather_kernel(own_ref, all_ref, local_sem, line_send, line_recv, group_send, group_recv, twin_send, twin_recv):
    y, c, z, x = spot()
    (x2, y2), (x3, y3), around, second, third, twin = partners()
    rows = own_ref.shape[0] // NC

    def cut(k):
        return pl.ds(k * rows, rows)

    def remote(src, dst, send_sem, recv_sem, target):
        return pltpu.make_async_remote_copy(
            src_ref=src, dst_ref=dst, send_sem=send_sem, recv_sem=recv_sem, device_id=target, device_id_type=MESH
        )

    def along(d, k):
        return remote(own_ref.at[cut(k)], all_ref.at[y, c, z, x, cut(k)], line_send.at[d - 1, k], line_recv.at[d - 1, k], around[d - 1])

    def along_in(d, k):
        return remote(own_ref.at[cut(k)], all_ref.at[y, c, (z + 4 - d) % 4, x, cut(k)], line_send.at[d - 1, k], line_recv.at[d - 1, k], around[d - 1])

    def square(core, j):
        yy, xx = ((y, x), (y2, x2), (y3, x3), (1 - y, 1 - x))[j]
        return all_ref.at[yy, core, :, xx]

    def hop(j, to, k, slot, landing):
        part = square(c, j).at[:, cut(k)]
        return remote(part, part, group_send.at[slot, k], group_recv.at[landing, k], to)

    def hop_in(landing, k):
        part = square(c, landing).at[:, cut(k)]
        return remote(part, part, group_send.at[0, k], group_recv.at[landing, k], twin)

    def share(j, k):
        part = square(c, j).at[:, cut(k)]
        yy, xx = ((y, x), (y2, x2), (y3, x3), (1 - y, 1 - x))[j]
        landing = (0, 2, 1, 3)[j]
        return remote(part, part, twin_send.at[j, k], twin_recv.at[landing, k], twin)

    def share_in(landing, k):
        yy, xx = ((y, x), (y2, x2), (y3, x3), (1 - y, 1 - x))[landing]
        part = all_ref.at[yy, 1 - c, :, xx, cut(k)]
        return remote(part, part, twin_send.at[0, k], twin_recv.at[landing, k], twin)

    keep = pltpu.make_async_copy(own_ref, all_ref.at[y, c, z, x], local_sem)
    keep.start()
    greet(around + [second, third, twin])
    for k in range(NC):
        for d in (1, 2, 3):
            along(d, k).start()
    keep.wait()
    for step in range(NC + 2):
        k = step
        if k < NC:
            for d in (1, 2, 3):
                along_in(d, k).wait_recv()
            hop(0, third, k, 0, 2).start()
            hop(0, second, k, 1, 1).start()
            share(0, k).start()
        k = step - 1
        if 0 <= k < NC:
            hop_in(1, k).wait_recv()
            hop(1, third, k, 2, 3).start()
            share(1, k).start()
        k = step - 2
        if 0 <= k < NC:
            hop_in(2, k).wait_recv()
            share(2, k).start()
            hop_in(3, k).wait_recv()
            share(3, k).start()
    for k in range(NC):
        for d in (1, 2, 3):
            along(d, k).wait_send()
        hop(0, third, k, 0, 2).wait_send()
        hop(0, second, k, 1, 1).wait_send()
        hop(1, third, k, 2, 3).wait_send()
        for j in range(4):
            share(j, k).wait_send()
            share_in(j, k).wait_recv()


def gather_packed(own):
    rows = own.shape[0]
    dma = pltpu.SemaphoreType.DMA
    return pl.pallas_call(
        gather_kernel,
        out_shape=jax.ShapeDtypeStruct((2, 2, 4, 2, rows, 128), own.dtype),
        in_specs=[pl.BlockSpec(memory_space=pl.ANY)],
        out_specs=pl.BlockSpec(memory_space=pl.ANY),
        scratch_shapes=[dma, dma((3, NC)), dma((3, NC)), dma((3, NC)), dma((4, NC)), dma((4, NC)), dma((4, NC))],
        compiler_params=pltpu.CompilerParams(collective_id=0, has_side_effects=True, vmem_limit_bytes=60 << 20),
        name="gather_packed",
    )(own)


def reduce_kernel(part_ref, sum_ref, own, twin_in, third_in, second_in, line_in, load_sem, twin_send, twin_recv, third_send, third_recv, second_send, second_recv, line_send, line_recv):
    f32, bf16 = jnp.float32, jnp.bfloat16
    y, c, z, x = spot()
    (x2, y2), (x3, y3), around, second, third, twin = partners()
    rows = sum_ref.shape[0] // NC

    def cut(k):
        return pl.ds(k * rows, rows)

    def remote(src, dst, send_sem, recv_sem, target):
        return pltpu.make_async_remote_copy(
            src_ref=src, dst_ref=dst, send_sem=send_sem, recv_sem=recv_sem, device_id=target, device_id_type=MESH
        )

    spots = ((1 - y, 1 - x), (y3, x3), (y2, x2), (y, x))
    turned = ((1 - y, 1 - x), (y2, x2), (y3, x3), (y, x))

    def load(j, k):
        yy, xx = spots[j]
        return pltpu.make_async_copy(part_ref.at[yy, c, :, xx, cut(k)], own.at[j, :, cut(k)], load_sem.at[j, k])

    def swap(j, k):
        yy, xx = turned[j]
        return remote(part_ref.at[yy, 1 - c, :, xx, cut(k)], twin_in.at[j, :, cut(k)], twin_send.at[j, k], twin_recv.at[j, k], twin)

    def to_third(j, k):
        return remote(own.at[j, :, cut(k)], third_in.at[j, :, cut(k)], third_send.at[j, k], third_recv.at[j, k], third)

    def to_second(k):
        return remote(own.at[2, :, cut(k)], second_in.at[:, cut(k)], second_send.at[k], second_recv.at[k], second)

    def to_line(d, k):
        return remote(own.at[3, (z + d) % 4, cut(k)], line_in.at[d - 1, cut(k)], line_send.at[d - 1, k], line_recv.at[d - 1, k], around[d - 1])

    for k in range(NC):
        for j in range(4):
            load(j, k).start()
    greet(around + [second, third, twin])
    for k in range(NC):
        for j in range(4):
            swap(j, k).start()

    def pair(j, k):
        load(j, k).wait()
        swap(j, k).wait_recv()
        return own[j, :, cut(k)].astype(f32) + twin_in[j, :, cut(k)].astype(f32)

    for step in range(NC + 3):
        k = step
        if k < NC:
            for j in (0, 1):
                own[j, :, cut(k)] = pair(j, k).astype(bf16)
                to_third(j, k).start()
        k = step - 1
        if 0 <= k < NC:
            held = pair(2, k)
            to_third(0, k).wait_recv()
            own[2, :, cut(k)] = (held + third_in[0, :, cut(k)].astype(f32)).astype(bf16)
            to_second(k).start()
        k = step - 2
        if 0 <= k < NC:
            held = pair(3, k)
            to_third(1, k).wait_recv()
            to_second(k).wait_recv()
            held += third_in[1, :, cut(k)].astype(f32) + second_in[:, cut(k)].astype(f32)
            own[3, :, cut(k)] = held.astype(bf16)
            for d in (1, 2, 3):
                to_line(d, k).start()
        k = step - 3
        if 0 <= k < NC:
            total = own[3, z, cut(k)].astype(f32)
            for d in (1, 2, 3):
                to_line(d, k).wait_recv()
                total += line_in[d - 1, cut(k)].astype(f32)
            sum_ref[cut(k)] = total
    for k in range(NC):
        for j in range(4):
            swap(j, k).wait_send()
        for j in (0, 1):
            to_third(j, k).wait_send()
        to_second(k).wait_send()
        for d in (1, 2, 3):
            to_line(d, k).wait_send()


def reduce_packed(part):
    rows = part.shape[-2]
    bf16 = jnp.bfloat16
    dma = pltpu.SemaphoreType.DMA
    return pl.pallas_call(
        reduce_kernel,
        out_shape=jax.ShapeDtypeStruct((rows, 128), jnp.float32),
        in_specs=[pl.BlockSpec(memory_space=pl.ANY)],
        out_specs=pl.BlockSpec(memory_space=pltpu.VMEM),
        scratch_shapes=[
            pltpu.VMEM((4, 4, rows, 128), bf16),
            pltpu.VMEM((4, 4, rows, 128), bf16),
            pltpu.VMEM((2, 4, rows, 128), bf16),
            pltpu.VMEM((4, rows, 128), bf16),
            pltpu.VMEM((3, rows, 128), bf16),
            dma((4, NC)), dma((4, NC)), dma((4, NC)), dma((2, NC)), dma((2, NC)), dma((NC,)), dma((NC,)), dma((3, NC)), dma((3, NC)),
        ],
        compiler_params=pltpu.CompilerParams(collective_id=1, has_side_effects=True, vmem_limit_bytes=56 << 20),
        name="reduce_packed",
    )(part)


def on_device(
    pixels,
    band_mask,
    wavelength,
    owner_order,
    rest_weight,
    rest_moment1,
    rest_moment2,
    fc_weight,
    fc_moment1,
    fc_moment2,
    cotangent,
):
    f32 = jnp.float32
    bf16 = jnp.bfloat16
    kernel_rate = float(E * PATCH * NB) ** (-0.5)
    groups = lax.axis_size("group")
    own_rows = rest_weight.shape[0]
    own_blocks = own_rows // 8
    fits = lax.axis_size("group") == 4 and lax.axis_size("img") == 8
    extra = -own_rows % 128
    slot_blocks = (own_rows + extra) // 8
    rest_low = jnp.pad(rest_weight.astype(bf16), ((0, extra), (0, 0)))
    if fits:
        gathered = gather_packed(rest_low)
    else:
        gathered = lax.all_gather(rest_low, ("group", "img"), axis=0, tiled=True)
    shards = gathered.size // ((own_rows + extra) * 128)
    gathered = gathered.reshape(shards, own_rows + extra, 128)
    total_blocks = owner_order.shape[0]
    slots = jnp.pad(
        owner_order.reshape(shards, own_blocks),
        ((0, 0), (0, slot_blocks - own_blocks)),
        constant_values=total_blocks,
    ).reshape(-1)
    unpacked = spread_packed(gathered, slots, total_blocks)
    weights = {entry[0]: matrix for entry, matrix in zip(matrices(), unpacked)}
    vectors = unpacked[-1].reshape(-1)
    at = 0
    for entry_name, extent in layout():
        if len(extent) == 1:
            weights[entry_name] = vectors[at : at + extent[0]]
            at += extent[0]
    block_vectors = jnp.pad(vectors[: 5 * D].reshape(5, D), ((0, 3), (0, 0)))
    hyper_names = [
        "h_query",
        "h_key",
        "h_value",
        "h_out",
        "h_ffin",
        "h_ffout",
        "hn1_gain",
        "hn1_shift",
        "hn2_gain",
        "hn2_shift",
    ]
    hyper_params = {entry_name: weights[entry_name].astype(f32) for entry_name in hyper_names}
    embedded = embed_waves(wavelength)

    def hyper_run(params_in):
        return hyper_layer(embedded, params_in)

    shaped, hyper_pull = jax.vjp(hyper_run, hyper_params)
    shaped_low = shaped.astype(bf16)
    band_width = E // groups
    group_id = lax.axis_index("group")
    own_shaped = lax.dynamic_slice_in_dim(shaped_low, group_id * band_width, band_width, 2)
    master = lax.all_gather(fc_weight.astype(bf16), "group", axis=0, tiled=True)
    group_shaped = lax.dynamic_index_in_dim(shaped_low, group_id, 0, keepdims=False)
    kernel_low = make_kernels(group_shaped, master)
    mask = jnp.repeat(band_mask.astype(f32), PATCH, axis=1)
    kernel_all = lax.all_gather(kernel_low, "img", axis=0, tiled=True)
    stream = embed_patches(pixels, mask, kernel_all)
    block_out, grad_low, block_vectors, *block_grads = block_pass(
        stream, cotangent, block_vectors, *(weights[entry[0]] for entry in matrices()[:4])
    )
    pixel_grad, kernel_grad = unembed_patches(pixels, mask, kernel_all, grad_low)
    kernel_grad_low = lax.psum_scatter(kernel_grad, "img", scatter_dimension=0, tiled=True)
    all_groups = lax.all_gather(kernel_grad_low[None], "group", axis=0, tiled=True)
    fc_new, fc_first, fc_second, shaped_part = master_update(
        all_groups,
        own_shaped.reshape(groups * NB, band_width),
        fc_weight,
        fc_moment1,
        fc_moment2,
        kernel_rate,
    )
    grad_shaped = lax.dynamic_update_slice_in_dim(
        jnp.zeros((groups, NB, E), f32),
        shaped_part.reshape(groups, NB, band_width),
        group_id * band_width,
        2,
    )
    (hyper_grads,) = hyper_pull(grad_shaped)
    given = list(block_grads) + [hyper_grads[entry[0]] for entry in matrices()[4:]]
    pieces = [block_vectors[:5].reshape(-1)]
    pieces += [hyper_grads[name] for name, extent in layout() if extent == (E,)]
    pieces.append(jnp.zeros((vector_rows()[1] * 128 - at,), f32))
    given.append(jnp.concatenate(pieces).reshape(-1, 128))
    joint_term = collect_packed(given, slots, total_blocks, shards, own_rows + extra)
    if fits:
        rest_grad = reduce_packed(joint_term.reshape(2, 2, 4, 2, own_rows + extra, 128))
    else:
        rest_grad = lax.psum_scatter(
            joint_term, ("group", "img"), scatter_dimension=0, tiled=False
        ).astype(f32)
    rest_grad = rest_grad[:own_rows]
    rest_new, rest_first, rest_second = adamw_step(
        rest_weight, rest_moment1, rest_moment2, rest_grad, rest_rate
    )
    return (block_out, pixel_grad, rest_new, rest_first, rest_second, fc_new, fc_first, fc_second)


def solution(mesh):
    placed = (
        P(("group", "img"), None, None),
        P(("group", "img"), None),
        P(),
        P(),
        P(("group", "img"), None),
        P(("group", "img"), None),
        P(("group", "img"), None),
        P("group", "img"),
        P("group", "img"),
        P("group", "img"),
        P(("group", "img"), None),
    )
    return jax.shard_map(
        on_device,
        mesh=mesh,
        in_specs=placed,
        out_specs=(
            P(("group", "img"), None),
            P(("group", "img"), None, None),
            P(("group", "img"), None),
            P(("group", "img"), None),
            P(("group", "img"), None),
            P("group", "img"),
            P("group", "img"),
            P("group", "img"),
        ),
        check_vma=False,
    )
```

time: 1720 us -> 843 us (0.49)
  waiting for transfers between devices: 1340 us -> 420 us
  Pallas kernels: 0 us -> 339 us
  local copies, waits for them, and re-layouts: 214 us -> 21 us
  matrix products: 114 us -> 23.3 us
  other arithmetic: 32.9 us -> 13.8 us
    unnamed x7 -> x4, waiting for transfers between devices: 603 us -> 0.07 us
    pallas_call x0 -> x9, Pallas kernels: none -> 339 us  [the longest x1 112 us: gather_packed(): pl.pallas_call(gather_kernel, out_shape=jax.ShapeDtypeStruct((2, 2, 4, 2,...]
    reduce_scatter x2 -> x1, waiting for transfers between devices: 456 us -> 205 us  [on_device(): lax.psum_scatter(kernel_grad, 'img', scatter_dimension=0, tiled=True)]
    dot_general x24 -> x0, matrix products: 88.2 us -> none  [the longest x1 12.1 us: on_device(): lax.dot_general(part_cols, masked, (((0,), (0,)), ((), ())), preferred_el...]
    all_gather x3, waiting for transfers between devices: 278 us -> 214 us  [the longest x1 171 us: on_device(): kernel_all = lax.all_gather(kernel_low, 'img', axis=0, tiled=True)]
    reshape x9 -> x5, local copies, waits for them, and re-layouts: 61.5 us -> 3.06 us  [the longest x1 1.33 us: on_device(): block_vectors = jnp.pad(vectors[:5 * D].reshape(5, D), ((0, 3), (0, 0)))]
    gather x2 -> x0, local copies, waits for them, and re-layouts: 50.1 us -> none  [the longest x1 27.4 us: on_device(): joint_term = grad_blocks[owner_order].reshape(-1, 128)]
    unnamed x196 -> x83, local copies, waits for them, and re-layouts: 57.3 us -> 7.94 us
  transfers between devices with their start and end apart: 6 -> 4, of which waited for: 6 -> 3; matrix products, arithmetic and copies ran while one was open for 9% -> 3% of each run, Pallas kernels for 0% -> 18%
where the time goes in v1:
time: 843 us; the launch traced here: 833 us
  waiting for transfers between devices  420 us (50%)
  Pallas kernels  339 us (40%)
  matrix products  23.3 us (3%)
  local copies, waits for them, and re-layouts  21 us (2%)
  between operations  15 us (2%)
  other arithmetic  13.8 us (2%)
    reduce_scatter x1, waiting for transfers between devices, on_device(): lax.psum_scatter(kernel_grad, 'img', scatter_dimension=0, tiled=True)  205 us
    all_gather x1, waiting for transfers between devices, on_device(): kernel_all = lax.all_gather(kernel_low, 'img', axis=0, tiled=True)  171 us
    pallas_call x1, Pallas kernels, gather_packed(): pl.pallas_call(gather_kernel, out_shape=jax.ShapeDtypeStruct((2, 2, 4, 2,...  112 us
    pallas_call x1, Pallas kernels, reduce_packed(): pl.pallas_call(reduce_kernel, out_shape=jax.ShapeDtypeStruct((rows, 128),...  79.7 us
    all_gather x1, waiting for transfers between devices, on_device(): lax.all_gather(kernel_grad_low[None], 'group', axis=0, tiled=True)  43.4 us
    pallas_call x1, Pallas kernels, spread_packed(): pl.pallas_call(spread_kernel, out_shape=shapes, grid_spec=pltpu.PrefetchS...  37.1 us
    pallas_call x1, Pallas kernels, collect_packed(): pl.pallas_call(collect_kernel, out_shape=jax.ShapeDtypeStruct((shards, ro...  32.4 us
    pallas_call x1, Pallas kernels, block_pass(): pl.pallas_call(block_kernel, out_shape=[jax.ShapeDtypeStruct((seq, D), bf...  31.3 us
  transfers between devices with their start and end apart: 4, of which 3 were waited for; matrix products, arithmetic and copies ran while one was open for 3% of the time, Pallas kernels for 18%

profile of v1, /device:TPU:0, one launch (start us, length us, event | category | flops | bytes accessed | tf_op | source)
XLA Modules:
  0.0 832.7 jit_solution(9203857727915204547)
XLA Ops:
  7.2 3.3 convert_element_type.26
  12.3 112.1 %gather_packed.1 = bf16[2,2,4,2,1920,128]{5,4,3,2,1,0:T(8,128)(2,1)} custom-call(bf16[1920,128]{1,0:T(8,128)(2,1)} %pad.13.own_ref), custom_call_target="tpu_custom_call" | custom-call | tf_op jit(solution)/shard_map/gather_packed/pallas_call | solution.py:690
  124.4 37.1 %spread_packed.1 = (bf16[768,2304]{1,0:T(8,128)(2,1)}, bf16[768,768]{1,0:T(8,128)(2,1)}, bf16[768,3072]{1,0:T(8,128)(2,1)}, bf16[3072,768]{1,0:T(8,128)(2,1)}, f...) custom-call(s32[7680]{0:T(1024)} %reshape.166.order_ref, ...), custom_call_target="tpu_custom_call" | custom-call | tf_op jit(solution)/shard_map/spread_packed/pallas_call | solution.py:109
  168.7 1.6 fusion.16
  170.3 2.3 fusion
  175.4 6.4 make_kernels.1
  182.1 1.3 slice.30
  184.8 1.3 reshape.172
  186.1 1.3 pad.14.vec_ref
  187.5 171.0 %all-gather.7.cloned.1.call-done.kernel_ref = bf16[768,8192]{1,0:T(8,128)(2,1)} async-done(((bf16[96,8192]{1,0:T(8,128)(2,1)}), bf16[768,8192]{1,0:T(8,128)(2,1)}) %all-gather.7.cloned.1.call-update) | async-done | bytes 12582928 | tf_op jit(solution)/shard_map/all_gather | solution.py:879
  358.5 11.0 %embed_patches.1.stream_ref = f32[196,768]{1,0:T(8,128)} custom-call(bf16[1,196,8192]{2,1,0:T(8,128)(2,1)} %pixel_ref.3, f32[1,8192]{1,0:T(1,128)} %bitcast.104, bf16[768,8192]{1,0:T(8,128)(2,1)} %all-gather.7.cloned.1.call-done.kernel_ref), custom_call_target="tpu_custom_call" | custom-call | tf_op jit(solution)/shard_map/embed_patches/pallas_call | solution.py:479
  369.5 31.3 %block_pass.1 = (bf16[196,768]{1,0:T(8,128)(2,1)}, bf16[208,768]{1,0:T(8,128)(2,1)}, f32[8,768]{1,0:T(8,128)}, bf16[768,2304]{1,0:T(8,128)(2,1)}, bf16[768,768]{...) custom-call(f32[196,768]{1,0:T(8,128)} %embed_patches.1.stream_ref, bf16[196,768]{1,0:T(8,128)(2,1)} %up_ref.1, ...), custom_call_target="tpu_custom_call" | custom-call | flops 8400000000 | bytes 30000000 | tf_op jit(solution)/shard_map/block_pass/pallas_call | solution.py:381
  400.9 16.1 %unembed_patches.1 = (bf16[1,196,8192]{2,1,0:T(8,128)(2,1)}, bf16[768,8192]{1,0:T(8,128)(2,1)}) custom-call(bf16[1,196,8192]{2,1,0:T(8,128)(2,1)} %pixel_ref.3, f32[1,8192]{1,0:T(1,128)} %bitcast.105, bf16[768,8192]{1,0:T(8,128)(2,1)} %all-gather.7.cloned.1.call-done.kernel_ref, bf16[208,768]{1,0:T(8,128)(2,1)} %get-tuple-element.44.low_ref), custom_call_target="tpu_custom_call" | custom-call | tf_op jit(solution)/shard_map/unembed_patches/pallas_call | solution.py:506
  417.3 205.3 %reduce-scatter.2.cloned.1.call-done = bf16[96,8192]{1,0:T(8,128)(2,1)} async-done(((bf16[768,8192]{1,0:T(8,128)(2,1)}), bf16[96,8192]{1,0:T(8,128)(2,1)}) %reduce-scatter.2.cloned.1.call-update) | async-done | bytes 1572880 | tf_op jit(solution)/shard_map/reduce_scatter | solution.py:885
  624.8 1.3 constant_dynamic-update-slice_fusion.5
  626.1 43.4 %all-gather.9.cloned.1.call-done = bf16[384,8192]{1,0:T(8,128)(2,1)} async-done(((bf16[96,8192]{1,0:T(8,128)(2,1)}), bf16[384,8192]{1,0:T(8,128)(2,1)}) %all-gather.9.cloned.1.call-update) | async-done | bytes 6291472 | tf_op jit(solution)/shard_map/all_gather | solution.py:886
  669.6 13.1 %master_update.1 = (f32[32,24576]{1,0:T(8,128)}, f32[32,24576]{1,0:T(8,128)}, f32[32,24576]{1,0:T(8,128)}, f32[128,32]{1,0:T(8,128)}) custom-call(bf16[4,96,8192]{2,1,0:T(8,128)(2,1)} %bitcast.99, bf16[128,32]{1,0:T(8,128)(2,1)} %bitcast.107, f32[32,24576]{1,0:T(8,128)} %weight_ref.1, f32[32,24576]{1,0:T(8,128)} %one_ref.1, f32[32,24576]{1,0:T(8,128)} %two_ref.1), custom_call_target="tpu_custom_call" | custom-call | tf_op jit(solution)/shard_map/master_update/pallas_call | solution.py:565
  683.3 1.5 dynamic_update_slice.3
  687.0 2.7 multiply_add_fusion
  689.7 2.8 convolution_bitcast_fusion.refs_9_
  693.7 2.1 convolution_bitcast_fusion.1.refs_8_
  709.9 32.4 %collect_packed.1 = bf16[32,1920,128]{2,1,0:T(8,128)(2,1)} custom-call(s32[7680]{0:T(1024)} %reshape.166.order_ref, bf16[768,2304]{1,0:T(8,128)(2,1)} %get-tuple-element.46.refs_0_, bf16[768,768]{1,0:T(8,128)(2,1)} %get-tuple-element.47.refs_1_, bf16[768,3072]{1,0:T(8,128)(2,1)} %get-tuple-element.48.refs_2_, bf16[3072,768]{1,0:T(8,128)(2,1)} %get-tuple-element.49.refs_3_, ...), custom_call_target="tpu_custom_call" | custom-call | tf_op jit(solution)/shard_map/collect_packed/pallas_call | solution.py:159
  742.4 79.7 %reduce_packed.1 = f32[1920,128]{1,0:T(8,128)} custom-call(bf16[2,2,4,2,1920,128]{5,4,3,2,1,0:T(8,128)(2,1)} %bitcast.97), custom_call_target="tpu_custom_call" | custom-call | tf_op jit(solution)/shard_map/reduce_packed/pallas_call | solution.py:790
  822.1 3.7 multiply_subtract_fusion
  (149 shorter events, 33.5 us)
Async XLA Ops:
  7.2 168.2 %all-gather.5.cloned.1.call-start = ((), (), s32[]{:S(2)}) async-start(), calls=%async_computation.1 | async-start | bytes 7864320 | tf_op jit(solution)/shard_map/all_gather | solution.py:875
  10.5 348.0 %all-gather.7.cloned.1.call-start = ((), (), s32[]{:S(2)}) async-start(), calls=%async_computation.2 | async-start | bytes 14155776 | tf_op jit(solution)/shard_map/all_gather | solution.py:879
  12.3 112.1 %copy-start.37 = (s32[4,32]{1,0:T(4,128)S(1)}, s32[4,32]{1,0:T(4,128)}, u32[]{:S(2)}) copy-start(s32[4,32]{1,0:T(4,128)} %param.13) | copy-start | bytes 1540
  161.4 5.6 copy-start.14
  161.4 7.3 copy-start.5
  163.1 5.6 copy-start.1
  167.0 5.6 copy-start.11
  167.9 6.0 copy-start.27
  167.9 6.0 copy-start.20
  168.7 6.0 copy-start.33
  181.9 440.7 %reduce-scatter.2.cloned.1.call-start = ((), (), s32[]{:S(2)}) async-start(), calls=%async_computation.3 | async-start | bytes 14155776 | tf_op jit(solution)/shard_map/reduce_scatter | solution.py:885
  417.0 252.5 %all-gather.9.cloned.1.call-start = ((), (), s32[]{:S(2)}) async-start(), calls=%async_computation.4 | async-start | bytes 7864320 | tf_op jit(solution)/shard_map/all_gather | solution.py:886
  669.6 15.3 %copy-start.19 = (f32[4,32]{1,0:T(4,128)S(1)}, f32[4,32]{1,0:T(4,128)}, u32[]{:S(2)}) copy-start(f32[4,32]{1,0:T(4,128)} %copy-done.18) | copy-start | bytes 1540
  669.6 15.3 %copy-start.23 = (f32[4,32]{1,0:T(4,128)S(1)}, f32[4,32]{1,0:T(4,128)}, u32[]{:S(2)}) copy-start(f32[4,32]{1,0:T(4,128)} %copy-done.22) | copy-start | bytes 1540
  669.6 15.3 %copy-start.34 = (f32[128]{0:T(128)S(1)}, f32[128]{0:T(128)}, u32[]{:S(2)}) copy-start(f32[128]{0:T(128)} %copy-done.33) | copy-start | bytes 1540
  669.6 16.3 %copy-start.30 = (f32[4,32]{1,0:T(4,128)S(1)}, f32[4,32]{1,0:T(4,128)}, u32[]{:S(2)}) copy-start(f32[4,32]{1,0:T(4,128)} %copy-done.29) | copy-start | bytes 1540
  686.9 5.6 copy-start.6
  686.9 5.6 copy-start.21
  689.7 6.1 copy-start.28
  689.7 6.3 copy-start.8
  692.5 5.6 copy-start.10
  692.6 6.1 copy-start.2
  742.4 79.7 %copy-start.12 = (f32[1880,128]{1,0:T(8,128)S(1)}, f32[1880,128]{1,0:T(8,128)}, u32[]{:S(2)}) copy-start(f32[1880,128]{1,0:T(8,128)} %param.16) | copy-start | bytes 2887684
  742.4 79.7 %copy-start.13 = (f32[1880,128]{1,0:T(8,128)S(1)}, f32[1880,128]{1,0:T(8,128)}, u32[]{:S(2)}) copy-start(f32[1880,128]{1,0:T(8,128)} %param.17) | copy-start | bytes 2887684
  (18 other events, 60.2 us)
Sparse Core Ops, SparseCore 0:
  10.6 74.9 all-gather.4
  182.0 176.4 all-gather.6
  417.1 205.4 reduce-scatter.1
  624.0 45.4 all-gather.8
